TPU v7x, 32 devices: a whole 2x2x4 slice. The times are simulated.
32 devices in a mesh: groups: 2 (over y), row: 2 (over x), col: 4 (over z), depth: 2 (over core).
Axes of the slice: x: 2, y: 2, z: 4, core: 2. Of those that a mesh axis runs over, the one named last changes fastest.
Arguments:
- layer_input: bfloat16 [4, 224, 4096], P(('groups', 'depth'), 'row', 'col'), parts along dimension 0, may hold values from -6 to 6
- out_grad: bfloat16 [4, 224, 4096], P(('groups', 'depth'), 'row', 'col'), parts along dimension 0, may hold values from -6 to 6
- gate_pre: bfloat16 [4, 224, 14336], P(('groups', 'depth'), 'col', 'row'), parts along dimension 0, may hold values from -6 to 6
- up_pre: bfloat16 [4, 224, 14336], P(('groups', 'depth'), 'col', 'row'), parts along dimension 0, may hold values from -6 to 6
- gate_weight: bfloat16 [4096, 14336], P('col', ('row', 'depth')), may hold values from -0.09375 to 0.09375
- up_weight: bfloat16 [4096, 14336], P('col', ('row', 'depth')), may hold values from -0.09375 to 0.09375
- down_weight: bfloat16 [14336, 4096], P(('row', 'depth'), 'col'), may hold values from -0.046875 to 0.046875
Outputs:
- input_grad: bfloat16 [4, 224, 4096], P(('groups', 'depth'), 'row', 'col'), parts along dimension 0
- gate_weight_grad: bfloat16 [4, 4096, 14336], P(('groups', 'depth'), 'col', 'row'), parts along dimension 0
- up_weight_grad: bfloat16 [4, 4096, 14336], P(('groups', 'depth'), 'col', 'row'), parts along dimension 0
- down_weight_grad: bfloat16 [4, 14336, 4096], P(('groups', 'depth'), 'row', 'col'), parts along dimension 0
There are 2 independent parts, one for each index of `groups`. A program takes and returns all parts, laid end to end along the dimension named above; an argument that names none is the same for every part. Nothing has to cross between parts.
All inputs are finite; a program needn't handle non-finite values.
Results may differ from a plain program's by a relative error of at most 0.03.
Values may be sent and summed in bfloat16 or wider, within the bound.
A program may use at most 192 MiB of HBM per device.

v0:
```python
import jax
import jax.numpy as jnp
from jax import lax
from jax.sharding import PartitionSpec as P


def swiglu_grads(hidden_grad, gate_rows, up_rows):
    gate_value = gate_rows.astype(jnp.float32)
    up_value = up_rows.astype(jnp.float32)
    sig = jax.nn.sigmoid(gate_value)
    silu_value = gate_value * sig
    hidden = (silu_value * up_value).astype(jnp.bfloat16)
    gate_grad = (hidden_grad * up_value * sig * (1.0 + gate_value * (1.0 - sig))).astype(
        jnp.bfloat16
    )
    up_grad = (hidden_grad * silu_value).astype(jnp.bfloat16)
    return (gate_grad, up_grad, hidden)


def times_transposed(left, right):
    return lax.dot_general(
        left, right, (((1,), (1,)), ((), ())), preferred_element_type=jnp.float32
    )


def over_tokens(left, right):
    return lax.dot_general(
        left, right, (((0,), (0,)), ((), ())), preferred_element_type=jnp.float32
    )


def shards(layer_input, out_grad, gate_pre, up_pre, gate_weight, up_weight, down_weight):
    gate_full, up_full, down_full = (
        lax.all_gather(gate_weight, "depth", axis=1, tiled=True),
        lax.all_gather(up_weight, "depth", axis=1, tiled=True),
        lax.all_gather(down_weight, "depth", axis=0, tiled=True),
    )
    input_rows, grad_rows = (
        lax.all_gather(layer_input[0], "row", axis=0, tiled=True),
        lax.all_gather(out_grad[0], "row", axis=0, tiled=True),
    )
    gate_rows, up_rows = (
        lax.all_gather(gate_pre[0], "col", axis=0, tiled=True),
        lax.all_gather(up_pre[0], "col", axis=0, tiled=True),
    )
    partial_hidden = times_transposed(grad_rows, down_full)
    hidden_grad = lax.psum(partial_hidden.astype(jnp.bfloat16), "col").astype(jnp.float32)
    gate_grad, up_grad, hidden = swiglu_grads(hidden_grad, gate_rows, up_rows)
    gate_wgrad = over_tokens(input_rows, gate_grad).astype(jnp.bfloat16)
    up_wgrad = over_tokens(input_rows, up_grad).astype(jnp.bfloat16)
    down_wgrad = over_tokens(hidden, grad_rows).astype(jnp.bfloat16)
    input_share = lax.psum_scatter(
        (times_transposed(gate_grad, gate_full) + times_transposed(up_grad, up_full)).astype(
            jnp.bfloat16
        ),
        "row",
        scatter_dimension=0,
        tiled=True,
    )
    return (input_share[None], gate_wgrad[None], up_wgrad[None], down_wgrad[None])


def solution(mesh):
    return jax.shard_map(
        shards,
        mesh=mesh,
        in_specs=(
            P(("groups", "depth"), "row", "col"),
            P(("groups", "depth"), "row", "col"),
            P(("groups", "depth"), "col", "row"),
            P(("groups", "depth"), "col", "row"),
            P("col", ("row", "depth")),
            P("col", ("row", "depth")),
            P(("row", "depth"), "col"),
        ),
        out_specs=(
            P(("groups", "depth"), "row", "col"),
            P(("groups", "depth"), "col", "row"),
            P(("groups", "depth"), "col", "row"),
            P(("groups", "depth"), "row", "col"),
        ),
        check_vma=False,
    )
```

profile of v0, /device:TPU:0, one launch (start us, length us, event | category | flops | bytes accessed | tf_op | source)
XLA Modules:
  0.0 433.5 jit_solution(16787232423276558372)
XLA Ops:
  7.2 0.0 copy-start.1
  7.2 0.0 all-gather.10.cloned.1.call-start
  7.2 0.7 all-gather.10.cloned.1.call-update
  7.9 0.0 all-gather.18.cloned.1.call-start
  8.0 0.7 all-gather.18.cloned.1.call-update
  8.7 0.0 all-gather.16.cloned.1.call-start
  8.7 0.7 all-gather.16.cloned.1.call-update
  9.4 0.0 all-reduce.2.cloned.1.call-start
  9.4 0.0 copy-done.1
  9.4 9.2 %all-gather = bf16[1,224,1024]{2,1,0:T(8,128)(2,1)S(1)} all-gather(bf16[1,112,1024]{2,1,0:T(8,128)(2,1)S(1)} %copy-done.1), channel_id=2, replica_groups=mesh['groups'=2,'row'=2,'col'=4,'depth'=2] {'row'}, dimensions={1}, use_global_device_ids=true | all-gather | bytes 688128 | tf_op jit(solution)/shard_map/all_gather | solution.py:40
  18.7 20.7 %all-gather.10.cloned.1.call-done = bf16[7168,1024]{1,0:T(8,128)(2,1)} async-done(((bf16[3584,1024]{1,0:T(8,128)(2,1)}), bf16[7168,1024]{1,0:T(8,128)(2,1)}) %all-gather.10.cloned.1.call-update) | async-done | bytes 14680080 | tf_op jit(solution)/shard_map/all_gather | solution.py:36
  39.3 15.9 %convolution_convert_fusion = bf16[224,7168]{1,0:T(8,128)(2,1)} fusion(bf16[7168,1024]{1,0:T(8,128)(2,1)} %all-gather.10.cloned.1.call-done, bf16[1,224,1024]{2,1,0:T(8,128)(2,1)S(1)} %all-gather), kind=kOutput, calls=%fused_computation.6 | convolution fusion | flops 3289939968 | bytes 18350080 | tf_op jit(solution)/shard_map/dot_general | solution.py:21
  55.3 0.0 all-reduce.2.cloned.1.call-update
  55.3 0.0 copy-start.2
  55.3 0.0 all-gather.12.cloned.1.call-start
  55.4 0.5 all-gather.12.cloned.1.call-update
  55.9 0.0 all-gather.14.cloned.1.call-start
  56.0 0.5 all-gather.14.cloned.1.call-update
  56.5 0.0 reduce-scatter.2.cloned.1.call-start
  56.5 0.0 copy-done.2
  56.5 8.7 %all-gather.3 = bf16[1,224,1024]{2,1,0:T(8,128)(2,1)} all-gather(bf16[1,112,1024]{2,1,0:T(8,128)(2,1)S(1)} %copy-done.2), channel_id=5, replica_groups=mesh['groups'=2,'row'=2,'col'=4,'depth'=2] {'row'}, dimensions={1}, use_global_device_ids=true | all-gather | bytes 688128 | tf_op jit(solution)/shard_map/all_gather | solution.py:39
  65.3 41.4 %all-gather.18.cloned.1.call-done = bf16[1,224,7168]{2,1,0:T(8,128)(2,1)} async-done(((bf16[1,56,7168]{2,1,0:T(8,128)(2,1)}), bf16[1,224,7168]{2,1,0:T(8,128)(2,1)}) %all-gather.18.cloned.1.call-update) | async-done | bytes 3211280 | tf_op jit(solution)/shard_map/all_gather | solution.py:43
  106.7 64.8 %all-gather.16.cloned.1.call-done = bf16[1,224,7168]{2,1,0:T(8,128)(2,1)} async-done(((bf16[1,56,7168]{2,1,0:T(8,128)(2,1)}), bf16[1,224,7168]{2,1,0:T(8,128)(2,1)}) %all-gather.16.cloned.1.call-update) | async-done | bytes 3211280 | tf_op jit(solution)/shard_map/all_gather | solution.py:44
  171.5 10.8 %convert_bitcast_fusion = bf16[1,7168,1024]{2,1,0:T(8,128)(2,1)} fusion(bf16[1,224,7168]{2,1,0:T(8,128)(2,1)} %all-gather.16.cloned.1.call-done, bf16[1,224,7168]{2,1,0:T(8,128)(2,1)} %all-gather.18.cloned.1.call-done, bf16[1,224,1024]{2,1,0:T(8,128)(2,1)S(1)} %all-gather), kind=kOutput, calls=%fused_computation | convolution fusion | flops 3308519424 | bytes 21561344 | tf_op jit(solution)/shard_map/dot_general | solution.py:27
  182.3 113.9 %all-reduce.2.cloned.1.call-done = bf16[224,7168]{1,0:T(8,128)(2,1)} async-done(((bf16[224,7168]{1,0:T(8,128)(2,1)}), bf16[224,7168]{1,0:T(8,128)(2,1)}) %all-reduce.2.cloned.1.call-update) | async-done | bytes 3211280 | tf_op jit(solution)/shard_map/psum | solution.py:47
  296.2 5.3 %fusion.3 = bf16[224,7168]{1,0:T(8,128)(2,1)S(1)} fusion(bf16[224,7168]{1,0:T(8,128)(2,1)} %all-reduce.2.cloned.1.call-done, bf16[1,224,7168]{2,1,0:T(8,128)(2,1)} %all-gather.16.cloned.1.call-done, bf16[1,224,7168]{2,1,0:T(8,128)(2,1)} %all-gather.18.cloned.1.call-done), kind=kLoop, calls=%fused_computation.13 | loop fusion | flops 20873216 | bytes 12845056 | tf_op jit(solution)/shard_map/convert_element_type | solution.py:13
  301.6 22.2 %all-gather.12.cloned.1.call-done = bf16[1024,7168]{1,0:T(8,128)(2,1)} async-done(((bf16[1024,3584]{1,0:T(8,128)(2,1)}), bf16[1024,7168]{1,0:T(8,128)(2,1)}) %all-gather.12.cloned.1.call-update) | async-done | bytes 14680080 | tf_op jit(solution)/shard_map/all_gather | solution.py:34
  323.8 8.7 %fusion.19 = f32[224,1024]{1,0:T(8,128)} fusion(bf16[224,7168]{1,0:T(8,128)(2,1)S(1)} %fusion.3, bf16[1024,7168]{1,0:T(8,128)(2,1)} %all-gather.12.cloned.1.call-done), kind=kOutput, calls=%fused_computation.27 | convolution fusion | flops 3288334336 | bytes 18808832 | tf_op jit(solution)/shard_map/dot_general | solution.py:21
  332.4 21.1 %all-gather.14.cloned.1.call-done = bf16[1024,7168]{1,0:T(8,128)(2,1)} async-done(((bf16[1024,3584]{1,0:T(8,128)(2,1)}), bf16[1024,7168]{1,0:T(8,128)(2,1)}) %all-gather.14.cloned.1.call-update) | async-done | bytes 14680080 | tf_op jit(solution)/shard_map/all_gather | solution.py:35
  353.5 12.8 %fusion.11 = bf16[224,1024]{1,0:T(8,128)(2,1)} fusion(f32[224,1024]{1,0:T(8,128)} %fusion.19, bf16[1024,7168]{1,0:T(8,128)(2,1)} %all-gather.14.cloned.1.call-done, bf16[224,7168]{1,0:T(8,128)(2,1)} %all-reduce.2.cloned.1.call-done, bf16[1,224,7168]{2,1,0:T(8,128)(2,1)} %all-gather.18.cloned.1.call-done), kind=kOutput, calls=%fused_computation.21 | convolution fusion | flops 3301638144 | bytes 22478848 | tf_op jit(solution)/shard_map/dot_general | solution.py:21
  366.3 0.0 reduce-scatter.2.cloned.1.call-update
  366.3 8.6 %convert_bitcast_fusion.2 = bf16[1,1024,7168]{1,2,0:T(8,128)(2,1)} fusion(bf16[224,7168]{1,0:T(8,128)(2,1)S(1)} %fusion.3, bf16[1,224,1024]{2,1,0:T(8,128)(2,1)} %all-gather.3), kind=kOutput, calls=%fused_computation.2 | convolution fusion | flops 3295674368 | bytes 18350080 | tf_op jit(solution)/shard_map/dot_general | solution.py:27
  374.9 0.0 copy-start
  374.9 20.1 %copy.11 = bf16[1,1024,7168]{2,1,0:T(8,128)(2,1)} copy(bf16[1,1024,7168]{1,2,0:T(8,128)(2,1)} %convert_bitcast_fusion.2) | data formatting | bytes 29360128
  395.0 0.0 copy-done
  395.0 11.7 %convert_bitcast_fusion.1 = bf16[1,1024,7168]{1,2,0:T(8,128)(2,1)} fusion(bf16[1,224,1024]{2,1,0:T(8,128)(2,1)} %all-gather.3, bf16[224,7168]{1,0:T(8,128)(2,1)} %all-reduce.2.cloned.1.call-done, bf16[1,224,7168]{2,1,0:T(8,128)(2,1)S(1)} %copy-done), kind=kOutput, calls=%fused_computation.1 | convolution fusion | flops 3308519424 | bytes 21561344 | tf_op jit(solution)/shard_map/dot_general | solution.py:27
  406.7 19.9 %copy.12 = bf16[1,1024,7168]{2,1,0:T(8,128)(2,1)} copy(bf16[1,1024,7168]{1,2,0:T(8,128)(2,1)} %convert_bitcast_fusion.1) | data formatting | bytes 29360128
  426.6 0.0 reduce-scatter.2.cloned.1.call-done
Async XLA Ops:
  7.2 2.3 copy-start.1
  7.2 32.2 %all-gather.10.cloned.1.call-start = ((), (), s32[]{:S(2)}) async-start(), calls=%async_computation.1 | async-start | bytes 22020096 | tf_op jit(solution)/shard_map/all_gather | solution.py:36
  7.9 98.8 %all-gather.18.cloned.1.call-start = ((), (), s32[]{:S(2)}) async-start(), calls=%async_computation.7 | async-start | bytes 4014080 | tf_op jit(solution)/shard_map/all_gather | solution.py:43
  8.7 162.9 %all-gather.16.cloned.1.call-start = ((), (), s32[]{:S(2)}) async-start(), calls=%async_computation.6 | async-start | bytes 4014080 | tf_op jit(solution)/shard_map/all_gather | solution.py:44
  9.4 286.8 %all-reduce.2.cloned.1.call-start = ((), (), s32[]{:S(2)}) async-start(), calls=%async_computation.2 | async-start | bytes 6422528 | tf_op jit(solution)/shard_map/psum | solution.py:47
  55.3 1.2 copy-start.2
  55.3 268.4 %all-gather.12.cloned.1.call-start = ((), (), s32[]{:S(2)}) async-start(), calls=%async_computation.3 | async-start | bytes 22020096 | tf_op jit(solution)/shard_map/all_gather | solution.py:34
  55.9 297.6 %all-gather.14.cloned.1.call-start = ((), (), s32[]{:S(2)}) async-start(), calls=%async_computation.4 | async-start | bytes 22020096 | tf_op jit(solution)/shard_map/all_gather | solution.py:35
  56.5 370.1 %reduce-scatter.2.cloned.1.call-start = ((), (), s32[]{:S(2)}) async-start(), calls=%async_computation.5 | async-start | bytes 688128 | tf_op jit(solution)/shard_map/reduce_scatter | solution.py:52
  374.9 20.1 %copy-start = (bf16[1,224,7168]{2,1,0:T(8,128)(2,1)S(1)}, bf16[1,224,7168]{2,1,0:T(8,128)(2,1)}, u32[]{:S(2)}) copy-start(bf16[1,224,7168]{2,1,0:T(8,128)(2,1)} %all-gather.18.cloned.1.call-done) | copy-start | bytes 9633796
Sparse Core Ops, SparseCore 0:
  9.6 29.7 all-gather.9
  40.9 65.7 all-gather.17
  108.3 63.2 all-gather.15
  174.3 121.8 all-reduce.1
  297.7 26.0 all-gather.11
  325.3 28.1 all-gather.13
  366.4 14.9 reduce-scatter.1
where the time goes:
time: 435 us; the launch traced here: 433 us
  waiting for transfers between devices  287 us (66%)
  matrix products  68.5 us (16%)
  local copies, waits for them, and re-layouts  40 us (9%)
  blocking collectives  17.9 us (4%)
  between operations  14.2 us (3%)
  other arithmetic  5.33 us (1%)
    psum x1, waiting for transfers between devices, shards(): lax.psum(partial_hidden.astype(jnp.bfloat16), 'col').astype(jnp.float32)  114 us
    all_gather x1, waiting for transfers between devices, shards(): lax.all_gather(up_pre[0], 'col', axis=0, tiled=True)  64.8 us
    all_gather x1, waiting for transfers between devices, shards(): lax.all_gather(gate_pre[0], 'col', axis=0, tiled=True)  41.4 us
    unnamed x8, local copies, waits for them, and re-layouts  40 us
    dot_general x3, matrix products, times_transposed(): lax.dot_general(left, right, (((1,), (1,)), ((), ())), preferred_element_...  37.4 us
    dot_general x3, matrix products, over_tokens(): lax.dot_general(left, right, (((0,), (0,)), ((), ())), preferred_element_...  31.2 us
    all_gather x1, waiting for transfers between devices, shards(): lax.all_gather(gate_weight, 'depth', axis=1, tiled=True)  22.2 us
    all_gather x1, waiting for transfers between devices, shards(): lax.all_gather(up_weight, 'depth', axis=1, tiled=True)  21.1 us
  transfers between devices with their start and end apart: 7, of which 6 were waited for; matrix products, arithmetic and copies ran while one was open for 23% of the time, Pallas kernels for 0%

commit v1 on v0

--- a/solution.py
+++ b/solution.py
@@ -2,6 +2,27 @@
 import jax.numpy as jnp
 from jax import lax
 from jax.sharding import PartitionSpec as P
+
+
+def collect(x, axis, dim):
+    devices, mine, rows = (lax.axis_size(axis), lax.axis_index(axis), x.shape[dim])
+    forward = [(i, (i + 1) % devices) for i in range(devices)]
+    left = [(i, (i - 1) % devices) for i in range(devices)]
+    out = jnp.zeros((*x.shape[:dim], devices * rows, *x.shape[dim + 1 :]), x.dtype)
+    out = lax.dynamic_update_slice_in_dim(out, x, mine * rows, axis=dim)
+    from_left = from_right = x
+    half = devices // 2
+    for hop in range(1, half + 1):
+        from_left = lax.ppermute(from_left, axis, forward)
+        out = lax.dynamic_update_slice_in_dim(
+            out, from_left, (mine - hop) % devices * rows, axis=dim
+        )
+        if hop < devices - half:
+            from_right = lax.ppermute(from_right, axis, left)
+            out = lax.dynamic_update_slice_in_dim(
+                out, from_right, (mine + hop) % devices * rows, axis=dim
+            )
+    return out
 
 
 def swiglu_grads(hidden_grad, gate_rows, up_rows):
@@ -41,7 +62,7 @@
     )
     gate_rows, up_rows = (
         lax.all_gather(gate_pre[0], "col", axis=0, tiled=True),
-        lax.all_gather(up_pre[0], "col", axis=0, tiled=True),
+        collect(up_pre[0], "col", 0),
     )
     partial_hidden = times_transposed(grad_rows, down_full)
     hidden_grad = lax.psum(partial_hidden.astype(jnp.bfloat16), "col").astype(jnp.float32)

time: 435 us -> 414 us (0.952)
  waiting for transfers between devices: 287 us -> 222 us
  starting transfers between devices: 0.27 us -> 36.6 us
  matrix products: 68.5 us -> 79.4 us
  other arithmetic: 5.33 us -> 0 us
    all_gather x1 -> x0, waiting for transfers between devices: 64.8 us -> none  [shards(): lax.all_gather(up_pre[0], 'col', axis=0, tiled=True)]
    ppermute x0 -> x3, waiting for transfers between devices: none -> 53.4 us  [the longest x2 53.3 us: collect(): from_left = lax.ppermute(from_left, axis, forward)]
    all_gather x1, waiting for transfers between devices: 41.4 us -> 0.02 us  [shards(): lax.all_gather(gate_pre[0], 'col', axis=0, tiled=True)]
    ppermute x0 -> x3, starting transfers between devices: none -> 36.4 us  [the longest x2 34.3 us: collect(): from_left = lax.ppermute(from_left, axis, forward)]
    all_gather x1, waiting for transfers between devices: 21.1 us -> 3.34 us  [shards(): lax.all_gather(up_weight, 'depth', axis=1, tiled=True)]
    psum x1, waiting for transfers between devices: 114 us -> 127 us  [shards(): lax.psum(partial_hidden.astype(jnp.bfloat16), 'col').astype(jnp.float32)]
    all_gather x1, waiting for transfers between devices: 22.2 us -> 14.2 us  [shards(): lax.all_gather(gate_weight, 'depth', axis=1, tiled=True)]
    dot_general x3, matrix products: 37.4 us -> 43.2 us  [times_transposed(): lax.dot_general(left, right, (((1,), (1,)), ((), ())), preferred_element_...]
  transfers between devices with their start and end apart: 7 -> 9, of which waited for: 6 -> 7; matrix products, arithmetic and copies ran while one was open for 23% -> 26% of each run, Pallas kernels for 0% -> 0%
where the time goes in v1:
time: 414 us; the launch traced here: 413 us
  waiting for transfers between devices  222 us (54%)
  matrix products  79.4 us (19%)
  local copies, waits for them, and re-layouts  43.9 us (11%)
  starting transfers between devices  36.6 us (9%)
  blocking collectives  17.4 us (4%)
  between operations  14.2 us (3%)
    psum x1, waiting for transfers between devices, shards(): lax.psum(partial_hidden.astype(jnp.bfloat16), 'col').astype(jnp.float32)  127 us
    ppermute x2, waiting for transfers between devices, collect(): from_left = lax.ppermute(from_left, axis, forward)  53.3 us
    dot_general x3, matrix products, times_transposed(): lax.dot_general(left, right, (((1,), (1,)), ((), ())), preferred_element_...  43.2 us
    unnamed x10, local copies, waits for them, and re-layouts  39.9 us
    dot_general x3, matrix products, over_tokens(): lax.dot_general(left, right, (((0,), (0,)), ((), ())), preferred_element_...  36.2 us
    ppermute x2, starting transfers between devices, collect(): from_left = lax.ppermute(from_left, axis, forward)  34.3 us
    all_gather x1, waiting for transfers between devices, shards(): lax.all_gather(down_weight, 'depth', axis=0, tiled=True)  20.7 us
    all_gather x1, waiting for transfers between devices, shards(): lax.all_gather(gate_weight, 'depth', axis=1, tiled=True)  14.2 us
  transfers between devices with their start and end apart: 9, of which 7 were waited for; matrix products, arithmetic and copies ran while one was open for 26% of the time, Pallas kernels for 0%

profile of v1, /device:TPU:0, one launch (start us, length us, event | category | flops | bytes accessed | tf_op | source)
XLA Modules:
  0.0 413.0 jit_solution(5712873314332326347)
XLA Ops:
  7.2 0.0 copy-start.2
  7.2 0.0 all-gather.8.cloned.1.call-start
  7.2 0.7 all-gather.8.cloned.1.call-update
  7.9 0.0 all-gather.14.cloned.1.call-start
  8.0 0.7 all-gather.14.cloned.1.call-update
  8.7 0.0 all-gather.12.cloned.1.call-start
  8.7 0.7 all-gather.12.cloned.1.call-update
  9.4 0.0 all-reduce.2.cloned.1.call-start
  9.4 0.0 copy-done.2
  9.4 9.2 %all-gather = bf16[1,224,1024]{2,1,0:T(8,128)(2,1)S(1)} all-gather(bf16[1,112,1024]{2,1,0:T(8,128)(2,1)S(1)} %copy-done.2), channel_id=2, replica_groups=mesh['groups'=2,'row'=2,'col'=4,'depth'=2] {'row'}, dimensions={1}, use_global_device_ids=true | all-gather | bytes 688128 | tf_op jit(solution)/shard_map/all_gather | solution.py:61
  18.7 0.0 copy-start
  18.7 20.7 %all-gather.8.cloned.1.call-done = bf16[7168,1024]{1,0:T(8,128)(2,1)} async-done(((bf16[3584,1024]{1,0:T(8,128)(2,1)}), bf16[7168,1024]{1,0:T(8,128)(2,1)}) %all-gather.8.cloned.1.call-update) | async-done | bytes 14680080 | tf_op jit(solution)/shard_map/all_gather | solution.py:57
  39.3 15.9 %convolution_convert_fusion = bf16[224,7168]{1,0:T(8,128)(2,1)} fusion(bf16[7168,1024]{1,0:T(8,128)(2,1)} %all-gather.8.cloned.1.call-done, bf16[1,224,1024]{2,1,0:T(8,128)(2,1)S(1)} %all-gather), kind=kOutput, calls=%fused_computation.6 | convolution fusion | flops 3289939968 | bytes 18350080 | tf_op jit(solution)/shard_map/dot_general | solution.py:42
  55.3 0.0 copy-done
  55.3 0.0 all-reduce.2.cloned.1.call-update
  55.3 0.0 copy-start.3
  55.3 0.0 all-gather.10.cloned.1.call-start
  55.4 0.5 all-gather.10.cloned.1.call-update
  55.9 0.0 reduce-scatter.2.cloned.1.call-start
  56.0 1.8 collective-permute-start
  57.8 2.1 collective-permute-start.1
  59.8 0.3 broadcast_in_dim.15
  60.2 1.2 constant_dynamic-update-slice_fusion.3
  61.5 0.0 copy-done.3
  61.5 8.1 %all-gather.2 = bf16[1,224,1024]{2,1,0:T(8,128)(2,1)} all-gather(bf16[1,112,1024]{2,1,0:T(8,128)(2,1)S(1)} %copy-done.3), channel_id=4, replica_groups=mesh['groups'=2,'row'=2,'col'=4,'depth'=2] {'row'}, dimensions={1}, use_global_device_ids=true | all-gather | bytes 688128 | tf_op jit(solution)/shard_map/all_gather | solution.py:60
  69.6 26.4 %collective-permute-done = bf16[56,7168]{1,0:T(8,128)(2,1)} collective-permute-done((bf16[56,7168]{1,0:T(8,128)(2,1)}, bf16[56,7168]{1,0:T(8,128)(2,1)}, u32[]{:S(2)}, u32[]{:S(2)}) %collective-permute-start) | collective-permute-done | bytes 802848 | tf_op jit(solution)/shard_map/ppermute | solution.py:16
  96.1 32.5 %collective-permute-start.2 = (bf16[56,7168]{1,0:T(8,128)(2,1)}, bf16[56,7168]{1,0:T(8,128)(2,1)S(1)}, u32[]{:S(2)}, u32[]{:S(2)}) collective-permute-start(bf16[56,7168]{1,0:T(8,128)(2,1)} %collective-permute-done), channel_id=1, source_target_pairs={{0,2},{2,4},{4,6},{6,0},{1,3},{3,5},{5,7},{7,1},{8,10},{10,12},{12... | collective-permute-start | bytes 2408456 | tf_op jit(solution)/shard_map/ppermute | solution.py:16
  128.6 1.2 constant_dynamic-update-slice_fusion.2
  129.8 0.1 collective-permute-done.1
  130.0 1.2 constant_dynamic-update-slice_fusion.1
  131.2 26.9 %collective-permute-done.2 = bf16[56,7168]{1,0:T(8,128)(2,1)S(1)} collective-permute-done((bf16[56,7168]{1,0:T(8,128)(2,1)}, bf16[56,7168]{1,0:T(8,128)(2,1)S(1)}, u32[]{:S(2)}, u32[]{:S(2)}) %collective-permute-start.2) | collective-permute-done | bytes 802848 | tf_op jit(solution)/shard_map/ppermute | solution.py:16
  158.0 0.1 constant_dynamic-update-slice_fusion
  158.1 0.0 all-gather.14.cloned.1.call-done
  158.1 13.6 %convert_bitcast_fusion = bf16[1,7168,1024]{2,1,0:T(8,128)(2,1)} fusion(bf16[224,7168]{1,0:T(8,128)(2,1)S(1)} %constant_dynamic-update-slice_fusion, bf16[1,224,7168]{2,1,0:T(8,128)(2,1)} %all-gather.14.cloned.1.call-done, bf16[1,224,1024]{2,1,0:T(8,128)(2,1)} %copy-done), kind=kOutput, calls=%fused_computation | convolution fusion | flops 3308519424 | bytes 21561344 | tf_op jit(solution)/shard_map/dot_general | solution.py:48
  171.7 3.3 all-gather.12.cloned.1.call-done
  175.1 127.2 %all-reduce.2.cloned.1.call-done = bf16[224,7168]{1,0:T(8,128)(2,1)} async-done(((bf16[224,7168]{1,0:T(8,128)(2,1)}), bf16[224,7168]{1,0:T(8,128)(2,1)}) %all-reduce.2.cloned.1.call-update) | async-done | bytes 3211280 | tf_op jit(solution)/shard_map/psum | solution.py:68
  302.3 13.4 %fusion.17 = f32[224,1024]{1,0:T(8,128)} fusion(bf16[1024,7168]{1,0:T(8,128)(2,1)} %all-gather.12.cloned.1.call-done, bf16[224,7168]{1,0:T(8,128)(2,1)} %all-reduce.2.cloned.1.call-done, bf16[1,224,7168]{2,1,0:T(8,128)(2,1)} %all-gather.14.cloned.1.call-done), kind=kOutput, calls=%fused_computation.30 | convolution fusion | flops 3301179392 | bytes 22020096 | tf_op jit(solution)/shard_map/dot_general | solution.py:42
  315.7 14.2 %all-gather.10.cloned.1.call-done = bf16[1024,7168]{1,0:T(8,128)(2,1)} async-done(((bf16[1024,3584]{1,0:T(8,128)(2,1)}), bf16[1024,7168]{1,0:T(8,128)(2,1)}) %all-gather.10.cloned.1.call-update) | async-done | bytes 14680080 | tf_op jit(solution)/shard_map/all_gather | solution.py:55
  329.9 13.9 %fusion.10 = bf16[224,1024]{1,0:T(8,128)(2,1)} fusion(f32[224,1024]{1,0:T(8,128)} %fusion.17, bf16[1024,7168]{1,0:T(8,128)(2,1)} %all-gather.10.cloned.1.call-done, bf16[224,7168]{1,0:T(8,128)(2,1)S(1)} %constant_dynamic-update-slice_fusion, bf16[224,7168]{1,0:T(8,128)(2,1)} %all-reduce.2.cloned.1.call-done, ...), kind=kOutput, calls=%fused_computation.20 | convolution fusion | flops 3309666304 | bytes 25690112 | tf_op jit(solution)/shard_map/dot_general | solution.py:42
  343.7 0.0 reduce-scatter.2.cloned.1.call-update
  343.8 11.7 %convert_bitcast_fusion.2 = bf16[1,1024,7168]{1,2,0:T(8,128)(2,1)} fusion(bf16[1,224,1024]{2,1,0:T(8,128)(2,1)} %all-gather.2, bf16[224,7168]{1,0:T(8,128)(2,1)S(1)} %constant_dynamic-update-slice_fusion, bf16[224,7168]{1,0:T(8,128)(2,1)} %all-reduce.2.cloned.1.call-done, bf16[1,224,7168]{2,1,0:T(8,128)(2,1)} %all-gather.14.cloned.1.call-done), kind=kOutput, calls=%fused_computation.2 | convolution fusion | flops 3316547584 | bytes 24772608 | tf_op jit(solution)/shard_map/dot_general | solution.py:48
  355.5 0.0 copy-start.1
  355.5 20.0 %copy.11 = bf16[1,1024,7168]{2,1,0:T(8,128)(2,1)} copy(bf16[1,1024,7168]{1,2,0:T(8,128)(2,1)} %convert_bitcast_fusion.2) | data formatting | bytes 29360128
  375.4 0.0 copy-done.1
  375.5 10.8 %convert_bitcast_fusion.1 = bf16[1,1024,7168]{1,2,0:T(8,128)(2,1)} fusion(bf16[1,224,1024]{2,1,0:T(8,128)(2,1)S(1)} %copy-done.1, bf16[224,7168]{1,0:T(8,128)(2,1)} %all-reduce.2.cloned.1.call-done, bf16[1,224,7168]{2,1,0:T(8,128)(2,1)} %all-gather.14.cloned.1.call-done), kind=kOutput, calls=%fused_computation.1 | convolution fusion | flops 3308519424 | bytes 21561344 | tf_op jit(solution)/shard_map/dot_general | solution.py:48
  386.3 19.9 %copy.12 = bf16[1,1024,7168]{2,1,0:T(8,128)(2,1)} copy(bf16[1,1024,7168]{1,2,0:T(8,128)(2,1)} %convert_bitcast_fusion.1) | data formatting | bytes 29360128
  406.2 0.0 reduce-scatter.2.cloned.1.call-done
Async XLA Ops:
  7.2 2.3 copy-start.2
  7.2 32.2 %all-gather.8.cloned.1.call-start = ((), (), s32[]{:S(2)}) async-start(), calls=%async_computation.1 | async-start | bytes 22020096 | tf_op jit(solution)/shard_map/all_gather | solution.py:57
  7.9 150.2 %all-gather.14.cloned.1.call-start = ((), (), s32[]{:S(2)}) async-start(), calls=%async_computation.6 | async-start | bytes 4014080 | tf_op jit(solution)/shard_map/all_gather | solution.py:64
  8.7 166.4 %all-gather.12.cloned.1.call-start = ((), (), s32[]{:S(2)}) async-start(), calls=%async_computation.4 | async-start | bytes 22020096 | tf_op jit(solution)/shard_map/all_gather | solution.py:56
  9.4 292.9 %all-reduce.2.cloned.1.call-start = ((), (), s32[]{:S(2)}) async-start(), calls=%async_computation.2 | async-start | bytes 6422528 | tf_op jit(solution)/shard_map/psum | solution.py:68
  18.7 36.6 %copy-start = (bf16[1,224,1024]{2,1,0:T(8,128)(2,1)}, bf16[1,224,1024]{2,1,0:T(8,128)(2,1)S(1)}, u32[]{:S(2)}) copy-start(bf16[1,224,1024]{2,1,0:T(8,128)(2,1)S(1)} %all-gather) | copy-start | bytes 1376260
  55.3 6.2 %copy-start.3 = (bf16[1,112,1024]{2,1,0:T(8,128)(2,1)S(1)}, bf16[1,112,1024]{2,1,0:T(8,128)(2,1)}, u32[]{:S(2)}) copy-start(bf16[1,112,1024]{2,1,0:T(8,128)(2,1)} %param.7) | copy-start | bytes 688132
  55.3 274.5 %all-gather.10.cloned.1.call-start = ((), (), s32[]{:S(2)}) async-start(), calls=%async_computation.3 | async-start | bytes 22020096 | tf_op jit(solution)/shard_map/all_gather | solution.py:55
  55.9 350.3 %reduce-scatter.2.cloned.1.call-start = ((), (), s32[]{:S(2)}) async-start(), calls=%async_computation.5 | async-start | bytes 688128 | tf_op jit(solution)/shard_map/reduce_scatter | solution.py:73
  56.0 40.1 %collective-permute-start = (bf16[56,7168]{1,0:T(8,128)(2,1)}, bf16[56,7168]{1,0:T(8,128)(2,1)}, u32[]{:S(2)}, u32[]{:S(2)}) collective-permute-start(bf16[56,7168]{1,0:T(8,128)(2,1)} %bitcast.1), channel_id=1, source_target_pairs={{0,2},{2,4},{4,6},{6,0},{1,3},{3,5},{5,7},{7,1},{8,10},{10,12},{12... | collective-permute-start | bytes 2408456 | tf_op jit(solution)/shard_map/ppermute | solution.py:16
  57.8 72.2 %collective-permute-start.1 = (bf16[56,7168]{1,0:T(8,128)(2,1)}, bf16[56,7168]{1,0:T(8,128)(2,1)}, u32[]{:S(2)}, u32[]{:S(2)}) collective-permute-start(bf16[56,7168]{1,0:T(8,128)(2,1)} %bitcast.1), channel_id=1, source_target_pairs={{0,6},{2,0},{4,2},{6,4},{1,7},{3,1},{5,3},{7,5},{8,14},{10,8},{12,... | collective-permute-start | bytes 2408456 | tf_op jit(solution)/shard_map/ppermute | solution.py:21
  96.1 62.0 %collective-permute-start.2 = (bf16[56,7168]{1,0:T(8,128)(2,1)}, bf16[56,7168]{1,0:T(8,128)(2,1)S(1)}, u32[]{:S(2)}, u32[]{:S(2)}) collective-permute-start(bf16[56,7168]{1,0:T(8,128)(2,1)} %collective-permute-done), channel_id=1, source_target_pairs={{0,2},{2,4},{4,6},{6,0},{1,3},{3,5},{5,7},{7,1},{8,10},{10,12},{12... | collective-permute-start | bytes 2408456 | tf_op jit(solution)/shard_map/ppermute | solution.py:16
  355.5 20.0 %copy-start.1 = (bf16[1,224,1024]{2,1,0:T(8,128)(2,1)S(1)}, bf16[1,224,1024]{2,1,0:T(8,128)(2,1)}, u32[]{:S(2)}) copy-start(bf16[1,224,1024]{2,1,0:T(8,128)(2,1)} %all-gather.2) | copy-start | bytes 1376260
Sparse Core Ops, SparseCore 0:
  9.6 29.7 all-gather.7
  40.9 106.3 all-gather.13
  148.9 26.1 all-gather.11
  177.9 124.3 all-reduce.1
  303.8 26.0 all-gather.9
  343.9 14.9 reduce-scatter.1
